TPU v7x, 128 devices: a whole 4x4x4 slice. The times are simulated.
128 devices in a mesh: segment: 4 (over x), seq: 32 (over z, y, core).
Axes of the slice: x: 4, y: 4, z: 4, core: 2. Of those that a mesh axis runs over, the one named last changes fastest.
Arguments:
- token_ids: int32 [256], P('seq'), may hold values from 0 to 511
- cached_len: int32 [2], replicated, may hold values from 128 to 786432
- embed: bfloat16 [512, 8192], P(None, 'seq'), may hold values from -6 to 6
- gain: float32 [4, 8192], P('segment'), may hold values from 0.1 to 1.9
- w_in: bfloat16 [4, 8192, 3, 8192], P('segment', None, None, 'seq'), may hold values from -0.0625 to 0.0625
- short_filter: float32 [4, 7, 3, 8192], P('segment', None, None, 'seq'), may hold values from -2.5 to 2.5
- long_filter: float32 [4, 128, 512], P('segment', None, 'seq'), may hold values from -0.5 to 0.5
- w_out: bfloat16 [4, 8192, 8192], P('segment', None, 'seq'), may hold values from -0.0625 to 0.0625
- short_cycle: bfloat16 [4, 2, 128, 3, 8192], P('segment', None, None, None, 'seq'), may hold values from -6 to 6
- long_cycle: bfloat16 [4, 2, 128, 8192], P('segment', None, None, 'seq'), may hold values from -6 to 6
Outputs:
- section_out: bfloat16 [4, 256, 8192], P('segment', None, 'seq')
- new_short_cycle: bfloat16 [4, 2, 128, 3, 8192], P('segment', None, None, None, 'seq')
- new_long_cycle: bfloat16 [4, 2, 128, 8192], P('segment', None, None, 'seq')
All inputs are finite; a program needn't handle non-finite values.
Results may differ from a plain program's by a relative error of at most 0.023.
Values may be sent and summed in bfloat16 or wider, within the bound.
A program may use at most 128 MiB of HBM per device.

v0:
```python
import jax
import jax.numpy as jnp
from jax import lax
from jax.sharding import PartitionSpec as P

D = 8192
G = 512
VOCAB = 512
SHORT = 7
LONG = 128
REQUESTS = 2


def from_behind(block, axis, distance):
    devices = range(lax.axis_size(axis))
    route = [(i - distance, i) for i in devices if i - distance in devices]
    return lax.ppermute(block, axis, route)


def cycle_rows(cycle, offset):
    doubled = jnp.concatenate([cycle, cycle], axis=0)
    return lax.dynamic_slice_in_dim(doubled, offset, cycle.shape[0], 0)


def local(
    token_ids,
    cached_len,
    embed,
    gain,
    w_in,
    short_filter,
    long_filter,
    w_out,
    short_cycle,
    long_cycle,
):
    my_segment = lax.axis_index("segment")
    segments = lax.axis_size("segment")
    ids_all = lax.all_gather(token_ids, "seq", axis=0, tiled=True)
    tokens = ids_all.shape[0]
    appended = tokens // REQUESTS
    channels = embed.shape[1]
    vocab_ids = jnp.arange(VOCAB, dtype=jnp.int32)
    one_hot = (ids_all[:, None] == vocab_ids[None, :]).astype(jnp.bfloat16)
    start_rows = jnp.dot(one_hot, embed, preferred_element_type=jnp.float32).astype(jnp.bfloat16)
    gain_row = gain[0]
    proj_in = w_in[0].reshape(D, 3 * channels)
    short_taps = short_filter[0]
    kernel = jnp.repeat(long_filter[0], D // G, axis=1)[::-1][:, None, :]
    proj_out = w_out[0]
    short_cache = short_cycle[0]
    long_cache = long_cycle[0]
    every_request = list(range(REQUESTS))
    current = start_rows
    result_rows = jnp.zeros_like(start_rows)
    short_result = short_cache
    long_result = long_cache
    for turn_number in range(segments):
        number = len(every_request)
        gathered = lax.all_gather(current, "seq", axis=1, tiled=True)
        widened = gathered.astype(jnp.float32)
        scaling = lax.rsqrt(jnp.mean(widened * widened, axis=1, keepdims=True) + 1e-06)
        normed = (widened * scaling * gain_row[None, :]).astype(jnp.bfloat16)
        projected = jnp.dot(normed, proj_in, preferred_element_type=jnp.float32)
        projected = projected.astype(jnp.bfloat16).reshape(number * appended, 3, channels)
        mixed_parts = []
        short_cycles = []
        long_cycles = []
        for position, request in enumerate(every_request):
            prefix = lax.dynamic_index_in_dim(cached_len, request, 0, keepdims=False)
            own_rows = projected[position * appended : (position + 1) * appended]
            short_old = lax.dynamic_index_in_dim(short_cache, request, 0, keepdims=False)
            long_old = lax.dynamic_index_in_dim(long_cache, request, 0, keepdims=False)
            extended = jnp.concatenate([cycle_rows(short_old, prefix % LONG), own_rows], axis=0)
            wide_ext = extended.astype(jnp.float32)
            filtered = jnp.zeros((appended, 3, channels), jnp.float32)
            for tap_index in range(SHORT):
                filtered = (
                    filtered
                    + short_taps[tap_index][None]
                    * wide_ext[LONG - tap_index : LONG - tap_index + appended]
                )
            product = (filtered[:, 1] * filtered[:, 2]).astype(jnp.bfloat16)
            carried = jnp.concatenate([cycle_rows(long_old, prefix % LONG), product], axis=0)
            convolved = lax.conv_general_dilated(
                carried[1:].astype(jnp.float32)[None],
                kernel,
                window_strides=(1,),
                padding="VALID",
                dimension_numbers=("NWC", "WIO", "NWC"),
                feature_group_count=channels,
                precision=lax.Precision.HIGHEST,
            )[0]
            mixed_parts.append((filtered[:, 0] * convolved).astype(jnp.bfloat16))
            backward = (LONG - (prefix + appended) % LONG) % LONG
            short_cycles.append(cycle_rows(extended[appended:], backward))
            long_cycles.append(cycle_rows(carried[appended:], backward))
        mixed = jnp.concatenate(mixed_parts, axis=0)
        initial = jnp.zeros((number * appended, channels), jnp.float32)
        shard_piece = lax.all_gather(mixed, "seq", axis=1, tiled=True)
        weight_rows = lax.slice_in_dim(proj_out, 0, shard_piece.shape[1], axis=0)
        summed = initial + jnp.dot(shard_piece, weight_rows, preferred_element_type=jnp.float32)
        output_rows = (current.astype(jnp.float32) + summed).astype(jnp.bfloat16)
        output_rows, short_cycles, long_cycles = (output_rows, short_cycles, long_cycles)
        is_mine = my_segment == turn_number
        result_rows = jnp.where(is_mine, output_rows, result_rows)
        short_result = jnp.where(is_mine, jnp.stack(short_cycles), short_result)
        long_result = jnp.where(is_mine, jnp.stack(long_cycles), long_result)
        if turn_number + 1 < segments:
            received = from_behind(output_rows, "segment", 1)
            current = jnp.where(my_segment == 0, start_rows, received)
    return (result_rows[None], short_result[None], long_result[None])


def solution(mesh):
    in_specs = (
        P("seq"),
        P(),
        P(None, "seq"),
        P("segment", None),
        P("segment", None, None, "seq"),
        P("segment", None, None, "seq"),
        P("segment", None, "seq"),
        P("segment", None, "seq"),
        P("segment", None, None, None, "seq"),
        P("segment", None, None, "seq"),
    )
    out_specs = (
        P("segment", None, "seq"),
        P("segment", None, None, None, "seq"),
        P("segment", None, None, "seq"),
    )
    return jax.shard_map(local, mesh=mesh, in_specs=in_specs, out_specs=out_specs, check_vma=False)
```

profile of v0, /device:TPU:1, one launch (start us, length us, event | category | flops | bytes accessed | tf_op | source)
XLA Modules:
  0.0 538.5 jit_solution(9733577705821494347)
XLA Ops:
  7.2 1.3 dynamic-slice.4
  9.2 0.9 dynamic-update-slice
  10.0 15.7 %all-reduce = s32[256]{0:T(256)S(1)} all-reduce(s32[256]{0:T(256)S(1)} %dynamic-update-slice), channel_id=1, replica_groups=mesh['segment'=4,'seq'=32] {'seq'}, use_global_device_ids=true, to_apply=%add | all-reduce | flops 256 | bytes 2048
  25.8 0.9 convolution_convert_fusion
  26.8 1.4 fusion.202
  32.1 16.7 %copy.58 = bf16[1,8192,3,256]{1,3,2,0:T(8,128)(2,1)} copy(bf16[1,8192,3,256]{3,1,2,0:T(8,128)(2,1)} %param.14) | data formatting | bytes 25165824 | tf_op args[4]
  50.2 26.2 %all-gather.9.cloned.1.call-done = bf16[256,8192]{1,0:T(8,128)(2,1)} async-done(((bf16[256,256]{1,0:T(8,128)(2,1)}), bf16[256,8192]{1,0:T(8,128)(2,1)}) %all-gather.9.cloned.1.call-update) | async-done | bytes 4194320 | tf_op jit(solution)/shard_map/all_gather | solution.py:60
  76.3 3.3 fusion
  79.8 8.2 %fusion.36 = bf16[256,768]{1,0:T(8,128)(2,1)S(1)} fusion(bf16[8192,768]{0,1:T(8,128)(2,1)} %bitcast.197, bf16[256,8192]{1,0:T(8,128)(2,1)S(1)} %copy-done.2, f32[8192]{0:T(1024)S(1)} %bitcast.236, f32[256]{0:T(256)S(1)} %add_rsqrt_fusion.3), kind=kOutput, calls=%fused_computation.40 | convolution fusion | flops 3229810688 | bytes 17204224 | tf_op jit(solution)/shard_map/dot_general | solution.py:64
  88.9 1.4 fusion.125
  91.1 1.4 fusion.123
  92.6 0.7 pad_maximum_fusion.16
  93.3 48.9 %all-gather.11.cloned.1.call-done = bf16[256,8192]{1,0:T(8,128)(2,1)} async-done(((bf16[256,256]{1,0:T(8,128)(2,1)}), bf16[256,8192]{1,0:T(8,128)(2,1)}) %all-gather.11.cloned.1.call-update) | async-done | bytes 4194320 | tf_op jit(solution)/shard_map/all_gather | solution.py:100
  142.2 4.7 fusion.51
  146.9 3.1 collective-permute-start
  150.1 2.6 collective-permute-done
  152.7 0.7 broadcast_select_fusion.2
  153.7 50.4 %all-gather.13.cloned.1.call-done = bf16[256,8192]{1,0:T(8,128)(2,1)} async-done(((bf16[256,256]{1,0:T(8,128)(2,1)}), bf16[256,8192]{1,0:T(8,128)(2,1)}) %all-gather.13.cloned.1.call-update) | async-done | bytes 4194320 | tf_op jit(solution)/shard_map/all_gather | solution.py:60
  204.2 3.3 fusion.3
  207.6 8.2 %fusion.39 = bf16[256,768]{1,0:T(8,128)(2,1)S(1)} fusion(bf16[8192,768]{0,1:T(8,128)(2,1)} %bitcast.198, bf16[256,8192]{1,0:T(8,128)(2,1)S(1)} %copy-done.4, f32[256]{0:T(256)S(1)} %add_rsqrt_fusion.2, f32[8192]{0:T(1024)S(1)} %bitcast.237), kind=kOutput, calls=%fused_computation.41 | convolution fusion | flops 3229810688 | bytes 17204224 | tf_op jit(solution)/shard_map/dot_general | solution.py:64
  216.7 1.4 fusion.121
  218.9 1.4 fusion.119
  220.4 0.7 pad_maximum_fusion.17
  221.1 48.9 %all-gather.15.cloned.1.call-done = bf16[256,8192]{1,0:T(8,128)(2,1)} async-done(((bf16[256,256]{1,0:T(8,128)(2,1)}), bf16[256,8192]{1,0:T(8,128)(2,1)}) %all-gather.15.cloned.1.call-update) | async-done | bytes 4194320 | tf_op jit(solution)/shard_map/all_gather | solution.py:100
  270.0 4.7 add_convert_fusion.2
  274.8 3.1 collective-permute-start.1
  277.9 2.6 collective-permute-done.1
  280.5 0.7 broadcast_select_fusion.1
  281.8 50.2 %all-gather.17.cloned.1.call-done = bf16[256,8192]{1,0:T(8,128)(2,1)} async-done(((bf16[256,256]{1,0:T(8,128)(2,1)}), bf16[256,8192]{1,0:T(8,128)(2,1)}) %all-gather.17.cloned.1.call-update) | async-done | bytes 4194320 | tf_op jit(solution)/shard_map/all_gather | solution.py:60
  332.0 3.3 fusion.6
  335.4 8.2 %fusion.42 = bf16[256,768]{1,0:T(8,128)(2,1)S(1)} fusion(bf16[8192,768]{0,1:T(8,128)(2,1)} %bitcast.199, bf16[256,8192]{1,0:T(8,128)(2,1)S(1)} %copy-done.5, f32[256]{0:T(256)S(1)} %add_rsqrt_fusion.1, f32[8192]{0:T(1024)S(1)} %bitcast.238), kind=kOutput, calls=%fused_computation.42 | convolution fusion | flops 3229810688 | bytes 17204224 | tf_op jit(solution)/shard_map/dot_general | solution.py:64
  344.5 1.4 fusion.117
  346.9 1.4 fusion.115
  349.0 48.9 %all-gather.19.cloned.1.call-done = bf16[256,8192]{1,0:T(8,128)(2,1)} async-done(((bf16[256,256]{1,0:T(8,128)(2,1)}), bf16[256,8192]{1,0:T(8,128)(2,1)}) %all-gather.19.cloned.1.call-update) | async-done | bytes 4194320 | tf_op jit(solution)/shard_map/all_gather | solution.py:100
  397.9 4.7 add_convert_fusion.1
  402.7 3.1 collective-permute-start.2
  405.8 2.6 collective-permute-done.2
  408.4 0.7 broadcast_select_fusion
  409.3 50.6 %all-gather.21.cloned.1.call-done = bf16[256,8192]{1,0:T(8,128)(2,1)} async-done(((bf16[256,256]{1,0:T(8,128)(2,1)}), bf16[256,8192]{1,0:T(8,128)(2,1)}) %all-gather.21.cloned.1.call-update) | async-done | bytes 4194320 | tf_op jit(solution)/shard_map/all_gather | solution.py:60
  459.9 3.3 fusion.9
  463.3 8.2 %fusion.45 = bf16[256,768]{1,0:T(8,128)(2,1)S(1)} fusion(bf16[8192,768]{0,1:T(8,128)(2,1)} %bitcast.200, bf16[256,8192]{1,0:T(8,128)(2,1)S(1)} %copy-done.3, f32[256]{0:T(256)S(1)} %add_rsqrt_fusion, f32[8192]{0:T(1024)S(1)} %bitcast.239), kind=kOutput, calls=%fused_computation.43 | convolution fusion | flops 3229810688 | bytes 17204224 | tf_op jit(solution)/shard_map/dot_general | solution.py:64
  473.2 1.6 fusion.113
  474.9 1.4 fusion.111
  476.3 0.7 pad_maximum_fusion.19
  482.6 0.7 maximum_select_fusion.4
  483.3 0.9 maximum_select_fusion
  484.2 41.8 %all-gather.23.cloned.1.call-done = bf16[256,8192]{1,0:T(8,128)(2,1)} async-done(((bf16[256,256]{1,0:T(8,128)(2,1)}), bf16[256,8192]{1,0:T(8,128)(2,1)}) %all-gather.23.cloned.1.call-update) | async-done | bytes 4194320 | tf_op jit(solution)/shard_map/all_gather | solution.py:100
  526.0 5.4 %fusion.146 = bf16[1,256,256]{2,1,0:T(8,128)(2,1)} fusion(bf16[256,256]{1,0:T(8,128)(2,1)S(1)} %copy-done.8, bf16[256,256]{1,0:T(8,128)(2,1)} %copy-done.23, bf16[256,256]{1,0:T(8,128)(2,1)S(1)} %copy-done.22, bf16[256,256]{1,0:T(8,128)(2,1)S(1)} %copy-done.20, pred[]{:T(512)S(6)} %eq.67, pred[]{:T(512)S(6)} %eq.66, pred[]{:T(512)S(6)} %eq.62, ...), kind=kOutput, calls=%fused_computation.241 | convolution fusion | flops 1074200576 | bytes 9043972 | tf_op jit(solution)/shard_map/dot_general | solution.py:102
  (168 shorter events, 14.6 us)
Async XLA Ops:
  7.2 18.6 %copy-start = (bf16[512,256]{1,0:T(8,128)(2,1)S(1)}, bf16[512,256]{1,0:T(8,128)(2,1)}, u32[]{:S(2)}) copy-start(bf16[512,256]{1,0:T(8,128)(2,1)} %param.12) | copy-start | bytes 786436
  7.2 69.2 %all-gather.9.cloned.1.call-start = ((), (), s32[]{:S(2)}) async-start(), calls=%async_computation | async-start | bytes 4325376 | tf_op jit(solution)/shard_map/all_gather | solution.py:60
  26.7 115.5 %all-gather.11.cloned.1.call-start = ((), (), s32[]{:S(2)}) async-start(), calls=%async_computation.1 | async-start | bytes 4325376 | tf_op jit(solution)/shard_map/all_gather | solution.py:100
  32.1 16.8 %copy-start.17 = (f32[1,7,3,256]{3,0,2,1:T(1,128)S(1)}, f32[1,7,3,256]{3,0,2,1:T(1,128)}, u32[]{:S(2)}) copy-start(f32[1,7,3,256]{3,0,2,1:T(1,128)} %param.15) | copy-start | bytes 64516
  32.1 16.8 %copy-start.18 = (f32[1,128,16]{1,2,0:T(8,128)S(1)}, f32[1,128,16]{1,2,0:T(8,128)}, u32[]{:S(2)}) copy-start(f32[1,128,16]{1,2,0:T(8,128)} %param.16) | copy-start | bytes 24580
  32.1 17.2 %copy-start.11 = (bf16[1,2,128,256]{3,2,1,0:T(8,128)(2,1)S(1)}, bf16[1,2,128,256]{3,2,1,0:T(8,128)(2,1)}, u32[]{:S(2)}) copy-start(bf16[1,2,128,256]{3,2,1,0:T(8,128)(2,1)} %param.19) | copy-start | bytes 393220
  32.1 17.5 %copy-start.7 = (bf16[1,2,128,3,256]{4,2,3,1,0:T(8,128)(2,1)S(1)}, bf16[1,2,128,3,256]{4,2,3,1,0:T(8,128)(2,1)}, u32[]{:S(2)}) copy-start(bf16[1,2,128,3,256]{4,2,3,1,0:T(8,128)(2,1)} %param.18) | copy-start | bytes 1179652
  48.9 30.7 %copy-start.24 = (f32[1,8192]{1,0:T(1,128)S(1)}, f32[1,8192]{1,0:T(1,128)}, u32[]{:S(2)}) copy-start(f32[1,8192]{1,0:T(1,128)} %param.13) | copy-start | bytes 98308
  49.2 295.3 %copy-start.13 = (f32[128,1,256]{2,1,0:T(1,128)}, f32[128,1,256]{2,1,0:T(1,128)S(1)}, u32[]{:S(2)}) copy-start(f32[128,1,256]{2,1,0:T(1,128)S(1)} %copy.62) | copy-start | bytes 393220
  76.3 3.4 copy-start.2
  91.1 51.1 %copy-start.6 = (bf16[256,256]{1,0:T(8,128)(2,1)S(1)}, bf16[256,256]{1,0:T(8,128)(2,1)}, u32[]{:S(2)}) copy-start(bf16[256,256]{1,0:T(8,128)(2,1)} %convolution_convert_fusion) | copy-start | bytes 393220
  93.2 110.9 %all-gather.13.cloned.1.call-start = ((), (), s32[]{:S(2)}) async-start(), calls=%async_computation.2 | async-start | bytes 4325376 | tf_op jit(solution)/shard_map/all_gather | solution.py:60
  146.9 68.9 %copy-start.19 = (bf16[256,256]{1,0:T(8,128)(2,1)}, bf16[256,256]{1,0:T(8,128)(2,1)S(1)}, u32[]{:S(2)}) copy-start(bf16[256,256]{1,0:T(8,128)(2,1)S(1)} %fusion.51) | copy-start | bytes 393220
  146.9 5.7 %collective-permute-start = (bf16[256,256]{1,0:T(8,128)(2,1)S(1)}, bf16[256,256]{1,0:T(8,128)(2,1)S(1)}, u32[]{:S(2)}, u32[]{:S(2)}) collective-permute-start(bf16[256,256]{1,0:T(8,128)(2,1)S(1)} %fusion.51), channel_id=1, source_target_pairs={{0,32},{32,64},{64,96},{1,33},{33,65},{65,97},{2,34},{34,66},{66,9... | collective-permute-start | bytes 393224 | tf_op jit(solution)/shard_map/ppermute | solution.py:17
  153.4 116.7 %all-gather.15.cloned.1.call-start = ((), (), s32[]{:S(2)}) async-start(), calls=%async_computation.3 | async-start | bytes 4325376 | tf_op jit(solution)/shard_map/all_gather | solution.py:100
  204.2 3.4 copy-start.4
  218.9 51.1 %copy-start.9 = (bf16[256,256]{1,0:T(8,128)(2,1)S(1)}, bf16[256,256]{1,0:T(8,128)(2,1)}, u32[]{:S(2)}) copy-start(bf16[256,256]{1,0:T(8,128)(2,1)} %broadcast_select_fusion.2) | copy-start | bytes 393220
  221.1 110.9 %all-gather.17.cloned.1.call-start = ((), (), s32[]{:S(2)}) async-start(), calls=%async_computation.4 | async-start | bytes 4325376 | tf_op jit(solution)/shard_map/all_gather | solution.py:60
  274.8 68.9 %copy-start.21 = (bf16[256,256]{1,0:T(8,128)(2,1)}, bf16[256,256]{1,0:T(8,128)(2,1)S(1)}, u32[]{:S(2)}) copy-start(bf16[256,256]{1,0:T(8,128)(2,1)S(1)} %add_convert_fusion.2) | copy-start | bytes 393220
  274.8 5.7 %collective-permute-start.1 = (bf16[256,256]{1,0:T(8,128)(2,1)S(1)}, bf16[256,256]{1,0:T(8,128)(2,1)S(1)}, u32[]{:S(2)}, u32[]{:S(2)}) collective-permute-start(bf16[256,256]{1,0:T(8,128)(2,1)S(1)} %add_convert_fusion.2), channel_id=1, source_target_pairs={{0,32},{32,64},{64,96},{1,33},{33,65},{65,97},{2,34},{34,66},{66,9... | collective-permute-start | bytes 393224 | tf_op jit(solution)/shard_map/ppermute | solution.py:17
  281.2 116.7 %all-gather.19.cloned.1.call-start = ((), (), s32[]{:S(2)}) async-start(), calls=%async_computation.5 | async-start | bytes 4325376 | tf_op jit(solution)/shard_map/all_gather | solution.py:100
  332.0 3.4 copy-start.5
  345.9 0.9 copy-start.14
  346.9 51.1 %copy-start.10 = (bf16[256,256]{1,0:T(8,128)(2,1)S(1)}, bf16[256,256]{1,0:T(8,128)(2,1)}, u32[]{:S(2)}) copy-start(bf16[256,256]{1,0:T(8,128)(2,1)} %broadcast_select_fusion.1) | copy-start | bytes 393220
  349.0 110.9 %all-gather.21.cloned.1.call-start = ((), (), s32[]{:S(2)}) async-start(), calls=%async_computation.6 | async-start | bytes 4325376 | tf_op jit(solution)/shard_map/all_gather | solution.py:60
  402.7 60.5 %copy-start.23 = (bf16[256,256]{1,0:T(8,128)(2,1)}, bf16[256,256]{1,0:T(8,128)(2,1)S(1)}, u32[]{:S(2)}) copy-start(bf16[256,256]{1,0:T(8,128)(2,1)S(1)} %add_convert_fusion.1) | copy-start | bytes 393220
  402.7 5.7 %collective-permute-start.2 = (bf16[256,256]{1,0:T(8,128)(2,1)S(1)}, bf16[256,256]{1,0:T(8,128)(2,1)S(1)}, u32[]{:S(2)}, u32[]{:S(2)}) collective-permute-start(bf16[256,256]{1,0:T(8,128)(2,1)S(1)} %add_convert_fusion.1), channel_id=1, source_target_pairs={{0,32},{32,64},{64,96},{1,33},{33,65},{65,97},{2,34},{34,66},{66,9... | collective-permute-start | bytes 393224 | tf_op jit(solution)/shard_map/ppermute | solution.py:17
  409.1 116.9 %all-gather.23.cloned.1.call-start = ((), (), s32[]{:S(2)}) async-start(), calls=%async_computation.7 | async-start | bytes 4325376 | tf_op jit(solution)/shard_map/all_gather | solution.py:100
  459.9 3.4 copy-start.3
  472.0 1.2 copy-start.15
  473.2 1.7 copy-start.16
  476.3 6.3 %copy-start.12 = (bf16[1,2,128,256]{3,2,1,0:T(8,128)(2,1)S(1)}, bf16[1,2,128,256]{3,2,1,0:T(8,128)(2,1)}, u32[]{:S(2)}) copy-start(bf16[1,2,128,256]{3,2,1,0:T(8,128)(2,1)} %param.19) | copy-start | bytes 393220
  479.7 46.3 %copy-start.8 = (bf16[256,256]{1,0:T(8,128)(2,1)S(1)}, bf16[256,256]{1,0:T(8,128)(2,1)}, u32[]{:S(2)}) copy-start(bf16[256,256]{1,0:T(8,128)(2,1)} %broadcast_select_fusion) | copy-start | bytes 393220
  479.7 46.3 %copy-start.20 = (bf16[256,256]{1,0:T(8,128)(2,1)S(1)}, bf16[256,256]{1,0:T(8,128)(2,1)}, u32[]{:S(2)}) copy-start(bf16[256,256]{1,0:T(8,128)(2,1)} %copy-done.19) | copy-start | bytes 393220
  479.7 46.3 %copy-start.22 = (bf16[256,256]{1,0:T(8,128)(2,1)S(1)}, bf16[256,256]{1,0:T(8,128)(2,1)}, u32[]{:S(2)}) copy-start(bf16[256,256]{1,0:T(8,128)(2,1)} %copy-done.21) | copy-start | bytes 393220
  526.0 5.4 %copy-start.1 = (bf16[512,256]{1,0:T(8,128)(2,1)S(1)}, bf16[512,256]{1,0:T(8,128)(2,1)}, u32[]{:S(2)}) copy-start(bf16[512,256]{1,0:T(8,128)(2,1)} %param.12) | copy-start | bytes 786436
Sparse Core Ops, SparseCore 0:
  26.8 49.4 all-gather.8
  93.4 48.7 all-gather.10
  153.5 50.6 all-gather.12
  221.2 48.7 all-gather.14
  281.3 50.6 all-gather.16
  349.1 48.7 all-gather.18
  409.2 50.6 all-gather.20
  477.2 48.7 all-gather.22
where the time goes:
time: 547 us; the launch traced here: 538 us
  waiting for transfers between devices  374 us (68%)
  matrix products  64.9 us (12%)
  other arithmetic  26.7 us (5%)
  local copies, waits for them, and re-layouts  25.4 us (5%)
  between operations  21.3 us (4%)
  blocking collectives  15.7 us (3%)
  starting transfers between devices  10.6 us (2%)
    all_gather x4, waiting for transfers between devices, local(): shard_piece = lax.all_gather(mixed, 'seq', axis=1, tiled=True)  189 us
    all_gather x4, waiting for transfers between devices, local(): gathered = lax.all_gather(current, 'seq', axis=1, tiled=True)  177 us
    dot_general x4, matrix products, local(): projected = jnp.dot(normed, proj_in, preferred_element_type=jnp.float32)  33 us
    unnamed x58, local copies, waits for them, and re-layouts  19.8 us
    dot_general x4, matrix products, local(): jnp.dot(shard_piece, weight_rows, preferred_element_type=jnp.float32)  19.5 us
    unnamed x1, blocking collectives  15.7 us
    reduce_sum x4, other arithmetic, local(): jnp.mean(widened * widened, axis=1, keepdims=True) + 1e-06  13 us
    conv_general_dilated x8, matrix products, local(): lax.conv_general_dilated(carried[1:].astype(jnp.float32)[None], kernel, w...  11.5 us
  transfers between devices with their start and end apart: 11, of which 11 were waited for; matrix products, arithmetic and copies ran while one was open for 5% of the time, Pallas kernels for 0%

commit v1 on v0

--- a/solution.py
+++ b/solution.py
@@ -97,7 +97,16 @@
             long_cycles.append(cycle_rows(carried[appended:], backward))
         mixed = jnp.concatenate(mixed_parts, axis=0)
         initial = jnp.zeros((number * appended, channels), jnp.float32)
-        shard_piece = lax.all_gather(mixed, "seq", axis=1, tiled=True)
+        start_lots_all = lambda body: jnp.concatenate(
+            lax.all_to_all(
+                jnp.stack([body for _ in range(lax.axis_size("seq"))], 0),
+                axis_name="seq",
+                split_axis=0,
+                concat_axis=0,
+            ),
+            1,
+        )
+        shard_piece = start_lots_all(mixed)
         weight_rows = lax.slice_in_dim(proj_out, 0, shard_piece.shape[1], axis=0)
         summed = initial + jnp.dot(shard_piece, weight_rows, preferred_element_type=jnp.float32)
         output_rows = (current.astype(jnp.float32) + summed).astype(jnp.bfloat16)

time: 547 us -> 566 us (1.035)
  the two profiles are of different devices: /device:TPU:1 before, /device:TPU:0 now
where the time goes in v1:
time: 566 us; the launch traced here: 557 us
  waiting for transfers between devices  222 us (39%)
  blocking collectives  188 us (33%)
  matrix products  54.5 us (10%)
  local copies, waits for them, and re-layouts  29.7 us (5%)
  other arithmetic  24 us (4%)
  between operations  21.2 us (4%)
  starting transfers between devices  17 us (3%)
    all_to_all x3, blocking collectives, local(): lax.all_to_all(jnp.stack([body for _ in range(lax.axis_size('seq'))], 0),...  170 us
    all_gather x4, waiting for transfers between devices, local(): gathered = lax.all_gather(current, 'seq', axis=1, tiled=True)  167 us
    all_to_all x1, waiting for transfers between devices, local(): lax.all_to_all(jnp.stack([body for _ in range(lax.axis_size('seq'))], 0),...  46.2 us
    dot_general x4, matrix products, local(): projected = jnp.dot(normed, proj_in, preferred_element_type=jnp.float32)  33 us
    unnamed x64, local copies, waits for them, and re-layouts  19.9 us
    unnamed x1, blocking collectives  18.3 us
    reduce_sum x4, other arithmetic, local(): jnp.mean(widened * widened, axis=1, keepdims=True) + 1e-06  13 us
  transfers between devices with their start and end apart: 8, of which 8 were waited for; matrix products, arithmetic and copies ran while one was open for 4% of the time, Pallas kernels for 0%

profile of v1, /device:TPU:0, one launch (start us, length us, event | category | flops | bytes accessed | tf_op | source)
XLA Modules:
  0.0 556.6 jit_solution(495866418033696045)
XLA Ops:
  7.2 1.3 dynamic-slice.4
  9.2 0.9 dynamic-update-slice
  10.0 18.3 %all-reduce = s32[256]{0:T(256)S(1)} all-reduce(s32[256]{0:T(256)S(1)} %dynamic-update-slice), channel_id=1, replica_groups=mesh['segment'=4,'seq'=32] {'seq'}, use_global_device_ids=true, to_apply=%add | all-reduce | flops 256 | bytes 2048
  28.3 0.9 convolution_convert_fusion
  29.3 1.4 fusion.202
  34.7 16.8 %copy.62 = bf16[1,8192,3,256]{1,3,2,0:T(8,128)(2,1)} copy(bf16[1,8192,3,256]{3,1,2,0:T(8,128)(2,1)} %param.14) | data formatting | bytes 25165824 | tf_op args[4]
  52.8 22.3 %all-gather.5.cloned.1.call-done = bf16[256,8192]{1,0:T(8,128)(2,1)} async-done(((bf16[256,256]{1,0:T(8,128)(2,1)}), bf16[256,8192]{1,0:T(8,128)(2,1)}) %all-gather.5.cloned.1.call-update) | async-done | bytes 4194320 | tf_op jit(solution)/shard_map/all_gather | solution.py:60
  75.2 3.3 fusion
  78.6 8.2 %fusion.36 = bf16[256,768]{1,0:T(8,128)(2,1)S(1)} fusion(bf16[8192,768]{0,1:T(8,128)(2,1)} %bitcast.212, bf16[256,8192]{1,0:T(8,128)(2,1)S(1)} %copy-done.5, f32[8192]{0:T(1024)S(1)} %bitcast.251, f32[256]{0:T(256)S(1)} %add_rsqrt_fusion.3), kind=kOutput, calls=%fused_computation.40 | convolution fusion | flops 3229810688 | bytes 17204224 | tf_op jit(solution)/shard_map/dot_general | solution.py:64
  87.7 1.4 fusion.125
  89.9 1.4 fusion.123
  91.5 0.5 stack.56
  92.0 56.5 %all_to_all.20 = bf16[32,256,256]{1,2,0:T(8,128)(2,1)S(1)} all-to-all(bf16[32,256,256]{1,2,0:T(8,128)(2,1)S(1)} %stack.56), channel_id=1, replica_groups=mesh['segment'=4,'seq'=32] {'seq'}, dimensions={0} | all-to-all | bytes 8388608 | tf_op jit(solution)/shard_map/all_to_all | solution.py:101
  148.5 1.3 fusion.51
  149.8 3.9 collective-permute-start
  153.7 3.0 collective-permute-done
  156.7 0.7 broadcast_select_fusion.2
  157.5 48.4 %all-gather.7.cloned.1.call-done = bf16[256,8192]{1,0:T(8,128)(2,1)} async-done(((bf16[256,256]{1,0:T(8,128)(2,1)}), bf16[256,8192]{1,0:T(8,128)(2,1)}) %all-gather.7.cloned.1.call-update) | async-done | bytes 4194320 | tf_op jit(solution)/shard_map/all_gather | solution.py:60
  205.9 3.3 fusion.3
  209.3 8.2 %fusion.39 = bf16[256,768]{1,0:T(8,128)(2,1)S(1)} fusion(bf16[8192,768]{0,1:T(8,128)(2,1)} %bitcast.213, bf16[256,8192]{1,0:T(8,128)(2,1)S(1)} %copy-done.6, f32[256]{0:T(256)S(1)} %add_rsqrt_fusion.2, f32[8192]{0:T(1024)S(1)} %bitcast.252), kind=kOutput, calls=%fused_computation.41 | convolution fusion | flops 3229810688 | bytes 17204224 | tf_op jit(solution)/shard_map/dot_general | solution.py:64
  218.4 1.4 fusion.121
  220.6 1.4 fusion.119
  222.7 56.5 %all_to_all.21 = bf16[32,256,256]{1,2,0:T(8,128)(2,1)S(1)} all-to-all(bf16[32,256,256]{1,2,0:T(8,128)(2,1)S(1)} %stack.57), channel_id=1, replica_groups=mesh['segment'=4,'seq'=32] {'seq'}, dimensions={0} | all-to-all | bytes 8388608 | tf_op jit(solution)/shard_map/all_to_all | solution.py:101
  279.2 1.3 add_convert_fusion.2
  280.5 3.4 collective-permute-start.1
  283.9 3.0 collective-permute-done.1
  286.9 0.7 broadcast_select_fusion.1
  287.8 48.2 %all-gather.9.cloned.1.call-done = bf16[256,8192]{1,0:T(8,128)(2,1)} async-done(((bf16[256,256]{1,0:T(8,128)(2,1)}), bf16[256,8192]{1,0:T(8,128)(2,1)}) %all-gather.9.cloned.1.call-update) | async-done | bytes 4194320 | tf_op jit(solution)/shard_map/all_gather | solution.py:60
  336.0 3.3 fusion.6
  339.5 8.2 %fusion.42 = bf16[256,768]{1,0:T(8,128)(2,1)S(1)} fusion(bf16[8192,768]{0,1:T(8,128)(2,1)} %bitcast.214, bf16[256,8192]{1,0:T(8,128)(2,1)S(1)} %copy-done.7, f32[256]{0:T(256)S(1)} %add_rsqrt_fusion.1, f32[8192]{0:T(1024)S(1)} %bitcast.253), kind=kOutput, calls=%fused_computation.42 | convolution fusion | flops 3229810688 | bytes 17204224 | tf_op jit(solution)/shard_map/dot_general | solution.py:64
  348.6 1.4 fusion.117
  350.9 1.4 fusion.115
  352.9 56.5 %all_to_all.22 = bf16[32,256,256]{1,2,0:T(8,128)(2,1)S(1)} all-to-all(bf16[32,256,256]{1,2,0:T(8,128)(2,1)S(1)} %stack.58), channel_id=1, replica_groups=mesh['segment'=4,'seq'=32] {'seq'}, dimensions={0} | all-to-all | bytes 8388608 | tf_op jit(solution)/shard_map/all_to_all | solution.py:101
  409.4 1.3 add_convert_fusion.1
  410.8 3.6 collective-permute-start.2
  414.4 2.8 collective-permute-done.2
  417.1 0.7 broadcast_select_fusion
  417.8 48.4 %all-gather.11.cloned.1.call-done = bf16[256,8192]{1,0:T(8,128)(2,1)} async-done(((bf16[256,256]{1,0:T(8,128)(2,1)}), bf16[256,8192]{1,0:T(8,128)(2,1)}) %all-gather.11.cloned.1.call-update) | async-done | bytes 4194320 | tf_op jit(solution)/shard_map/all_gather | solution.py:60
  466.3 3.3 fusion.9
  469.7 8.2 %fusion.45 = bf16[256,768]{1,0:T(8,128)(2,1)S(1)} fusion(bf16[8192,768]{0,1:T(8,128)(2,1)} %bitcast.215, bf16[256,8192]{1,0:T(8,128)(2,1)S(1)} %copy-done.8, f32[256]{0:T(256)S(1)} %add_rsqrt_fusion, f32[8192]{0:T(1024)S(1)} %bitcast.254), kind=kOutput, calls=%fused_computation.43 | convolution fusion | flops 3229810688 | bytes 17204224 | tf_op jit(solution)/shard_map/dot_general | solution.py:64
  479.6 1.4 fusion.113
  481.0 1.4 fusion.111
  482.6 2.5 stack.59
  485.1 5.8 %all-to-all-start.3 = ((bf16[32,256,256]{1,2,0:T(8,128)(2,1)}), bf16[32,256,256]{1,2,0:T(8,128)(2,1)}, u32[]{:S(2)}, u32[]{:S(2)}) async-start(bf16[32,256,256]{1,2,0:T(8,128)(2,1)} %stack.59), calls=%async_computation.3 | async-start | bytes 8388608 | tf_op jit(solution)/shard_map/all_to_all | solution.py:101
  496.5 0.7 maximum_select_fusion.4
  497.3 0.9 maximum_select_fusion
  498.1 46.2 %all-to-all-done.3 = bf16[32,256,256]{1,2,0:T(8,128)(2,1)} async-done(((bf16[32,256,256]{1,2,0:T(8,128)(2,1)}), bf16[32,256,256]{1,2,0:T(8,128)(2,1)}, u32[]{:S(2)}, u32[]{:S(2)}) %all-to-all-start.3) | async-done | bytes 4194336 | tf_op jit(solution)/shard_map/all_to_all | solution.py:101
  544.4 5.5 fusion.146
  (175 shorter events, 14.3 us)
Async XLA Ops:
  7.2 21.1 %copy-start = (bf16[512,256]{1,0:T(8,128)(2,1)S(1)}, bf16[512,256]{1,0:T(8,128)(2,1)}, u32[]{:S(2)}) copy-start(bf16[512,256]{1,0:T(8,128)(2,1)} %param.12) | copy-start | bytes 786436
  7.2 68.0 %all-gather.5.cloned.1.call-start = ((), (), s32[]{:S(2)}) async-start(), calls=%async_computation.4 | async-start | bytes 4325376 | tf_op jit(solution)/shard_map/all_gather | solution.py:60
  29.3 176.6 %all-gather.7.cloned.1.call-start = ((), (), s32[]{:S(2)}) async-start(), calls=%async_computation.5 | async-start | bytes 4325376 | tf_op jit(solution)/shard_map/all_gather | solution.py:60
  34.7 16.8 %copy-start.25 = (f32[1,7,3,256]{3,0,2,1:T(1,128)S(1)}, f32[1,7,3,256]{3,0,2,1:T(1,128)}, u32[]{:S(2)}) copy-start(f32[1,7,3,256]{3,0,2,1:T(1,128)} %param.15) | copy-start | bytes 64516
  34.7 16.8 %copy-start.26 = (f32[1,128,16]{1,2,0:T(8,128)S(1)}, f32[1,128,16]{1,2,0:T(8,128)}, u32[]{:S(2)}) copy-start(f32[1,128,16]{1,2,0:T(8,128)} %param.16) | copy-start | bytes 24580
  34.7 17.2 %copy-start.20 = (bf16[1,2,128,256]{3,2,1,0:T(8,128)(2,1)S(1)}, bf16[1,2,128,256]{3,2,1,0:T(8,128)(2,1)}, u32[]{:S(2)}) copy-start(bf16[1,2,128,256]{3,2,1,0:T(8,128)(2,1)} %param.19) | copy-start | bytes 393220
  34.7 17.6 %copy-start.10 = (bf16[1,2,128,3,256]{4,2,3,1,0:T(8,128)(2,1)S(1)}, bf16[1,2,128,3,256]{4,2,3,1,0:T(8,128)(2,1)}, u32[]{:S(2)}) copy-start(bf16[1,2,128,3,256]{4,2,3,1,0:T(8,128)(2,1)} %param.18) | copy-start | bytes 1179652
  51.5 26.9 %copy-start.27 = (f32[1,8192]{1,0:T(1,128)S(1)}, f32[1,8192]{1,0:T(1,128)}, u32[]{:S(2)}) copy-start(f32[1,8192]{1,0:T(1,128)} %param.13) | copy-start | bytes 98308
  51.9 296.7 %copy-start.22 = (f32[128,1,256]{2,1,0:T(1,128)}, f32[128,1,256]{2,1,0:T(1,128)S(1)}, u32[]{:S(2)}) copy-start(f32[128,1,256]{2,1,0:T(1,128)S(1)} %copy.66) | copy-start | bytes 393220
  75.2 3.4 copy-start.5
  92.0 56.5 %copy-start.2 = (bf16[1,8192,256]{2,1,0:T(8,128)(2,1)S(1)}, bf16[1,8192,256]{2,1,0:T(8,128)(2,1)}, u32[]{:S(2)}) copy-start(bf16[1,8192,256]{2,1,0:T(8,128)(2,1)} %param.17) | copy-start | bytes 12582916
  92.0 56.5 %copy-start.9 = (bf16[256,256]{1,0:T(8,128)(2,1)S(1)}, bf16[256,256]{1,0:T(8,128)(2,1)}, u32[]{:S(2)}) copy-start(bf16[256,256]{1,0:T(8,128)(2,1)} %convolution_convert_fusion) | copy-start | bytes 393220
  149.8 67.7 %copy-start.14 = (bf16[256,256]{1,0:T(8,128)(2,1)}, bf16[256,256]{1,0:T(8,128)(2,1)S(1)}, u32[]{:S(2)}) copy-start(bf16[256,256]{1,0:T(8,128)(2,1)S(1)} %fusion.51) | copy-start | bytes 393220
  149.8 6.9 %collective-permute-start = (bf16[256,256]{1,0:T(8,128)(2,1)S(1)}, bf16[256,256]{1,0:T(8,128)(2,1)S(1)}, u32[]{:S(2)}, u32[]{:S(2)}) collective-permute-start(bf16[256,256]{1,0:T(8,128)(2,1)S(1)} %fusion.51), channel_id=1, source_target_pairs={{0,32},{32,64},{64,96},{1,33},{33,65},{65,97},{2,34},{34,66},{66,9... | collective-permute-start | bytes 393224 | tf_op jit(solution)/shard_map/ppermute | solution.py:17
  157.4 178.6 %all-gather.9.cloned.1.call-start = ((), (), s32[]{:S(2)}) async-start(), calls=%async_computation.6 | async-start | bytes 4325376 | tf_op jit(solution)/shard_map/all_gather | solution.py:60
  205.9 3.4 copy-start.6
  222.7 56.5 %copy-start.3 = (bf16[1,8192,256]{2,1,0:T(8,128)(2,1)S(1)}, bf16[1,8192,256]{2,1,0:T(8,128)(2,1)}, u32[]{:S(2)}) copy-start(bf16[1,8192,256]{2,1,0:T(8,128)(2,1)} %param.17) | copy-start | bytes 12582916
  222.7 56.5 %copy-start.12 = (bf16[256,256]{1,0:T(8,128)(2,1)S(1)}, bf16[256,256]{1,0:T(8,128)(2,1)}, u32[]{:S(2)}) copy-start(bf16[256,256]{1,0:T(8,128)(2,1)} %broadcast_select_fusion.2) | copy-start | bytes 393220
  280.5 67.2 %copy-start.16 = (bf16[256,256]{1,0:T(8,128)(2,1)}, bf16[256,256]{1,0:T(8,128)(2,1)S(1)}, u32[]{:S(2)}) copy-start(bf16[256,256]{1,0:T(8,128)(2,1)S(1)} %add_convert_fusion.2) | copy-start | bytes 393220
  280.5 6.4 %collective-permute-start.1 = (bf16[256,256]{1,0:T(8,128)(2,1)S(1)}, bf16[256,256]{1,0:T(8,128)(2,1)S(1)}, u32[]{:S(2)}, u32[]{:S(2)}) collective-permute-start(bf16[256,256]{1,0:T(8,128)(2,1)S(1)} %add_convert_fusion.2), channel_id=1, source_target_pairs={{0,32},{32,64},{64,96},{1,33},{33,65},{65,97},{2,34},{34,66},{66,9... | collective-permute-start | bytes 393224 | tf_op jit(solution)/shard_map/ppermute | solution.py:17
  287.6 178.7 %all-gather.11.cloned.1.call-start = ((), (), s32[]{:S(2)}) async-start(), calls=%async_computation.7 | async-start | bytes 4325376 | tf_op jit(solution)/shard_map/all_gather | solution.py:60
  336.0 3.4 copy-start.7
  350.0 0.9 copy-start.23
  352.9 56.5 %copy-start.4 = (bf16[1,8192,256]{2,1,0:T(8,128)(2,1)S(1)}, bf16[1,8192,256]{2,1,0:T(8,128)(2,1)}, u32[]{:S(2)}) copy-start(bf16[1,8192,256]{2,1,0:T(8,128)(2,1)} %param.17) | copy-start | bytes 12582916
  352.9 56.5 %copy-start.13 = (bf16[256,256]{1,0:T(8,128)(2,1)S(1)}, bf16[256,256]{1,0:T(8,128)(2,1)}, u32[]{:S(2)}) copy-start(bf16[256,256]{1,0:T(8,128)(2,1)} %broadcast_select_fusion.1) | copy-start | bytes 393220
  410.7 58.8 %copy-start.18 = (bf16[256,256]{1,0:T(8,128)(2,1)}, bf16[256,256]{1,0:T(8,128)(2,1)S(1)}, u32[]{:S(2)}) copy-start(bf16[256,256]{1,0:T(8,128)(2,1)S(1)} %add_convert_fusion.1) | copy-start | bytes 393220
  410.8 6.4 %collective-permute-start.2 = (bf16[256,256]{1,0:T(8,128)(2,1)S(1)}, bf16[256,256]{1,0:T(8,128)(2,1)S(1)}, u32[]{:S(2)}, u32[]{:S(2)}) collective-permute-start(bf16[256,256]{1,0:T(8,128)(2,1)S(1)} %add_convert_fusion.1), channel_id=1, source_target_pairs={{0,32},{32,64},{64,96},{1,33},{33,65},{65,97},{2,34},{34,66},{66,9... | collective-permute-start | bytes 393224 | tf_op jit(solution)/shard_map/ppermute | solution.py:17
  466.3 3.4 copy-start.8
  478.4 1.2 copy-start.24
  485.1 59.2 %all-to-all-start.3 = ((bf16[32,256,256]{1,2,0:T(8,128)(2,1)}), bf16[32,256,256]{1,2,0:T(8,128)(2,1)}, u32[]{:S(2)}, u32[]{:S(2)}) async-start(bf16[32,256,256]{1,2,0:T(8,128)(2,1)} %stack.59), calls=%async_computation.3 | async-start | bytes 8388608 | tf_op jit(solution)/shard_map/all_to_all | solution.py:101
  490.9 5.6 %copy-start.21 = (bf16[1,2,128,256]{3,2,1,0:T(8,128)(2,1)S(1)}, bf16[1,2,128,256]{3,2,1,0:T(8,128)(2,1)}, u32[]{:S(2)}) copy-start(bf16[1,2,128,256]{3,2,1,0:T(8,128)(2,1)} %param.19) | copy-start | bytes 393220
  493.6 50.8 %copy-start.11 = (bf16[256,256]{1,0:T(8,128)(2,1)S(1)}, bf16[256,256]{1,0:T(8,128)(2,1)}, u32[]{:S(2)}) copy-start(bf16[256,256]{1,0:T(8,128)(2,1)} %broadcast_select_fusion) | copy-start | bytes 393220
  493.6 50.7 %copy-start.15 = (bf16[256,256]{1,0:T(8,128)(2,1)S(1)}, bf16[256,256]{1,0:T(8,128)(2,1)}, u32[]{:S(2)}) copy-start(bf16[256,256]{1,0:T(8,128)(2,1)} %copy-done.14) | copy-start | bytes 393220
  493.6 50.7 %copy-start.17 = (bf16[256,256]{1,0:T(8,128)(2,1)S(1)}, bf16[256,256]{1,0:T(8,128)(2,1)}, u32[]{:S(2)}) copy-start(bf16[256,256]{1,0:T(8,128)(2,1)} %copy-done.16) | copy-start | bytes 393220
  493.6 50.7 %copy-start.19 = (bf16[256,256]{1,0:T(8,128)(2,1)S(1)}, bf16[256,256]{1,0:T(8,128)(2,1)}, u32[]{:S(2)}) copy-start(bf16[256,256]{1,0:T(8,128)(2,1)} %copy-done.18) | copy-start | bytes 393220
  544.3 5.5 copy-start.1
Sparse Core Ops, SparseCore 0:
  29.4 45.7 all-gather.4
  157.6 48.2 all-gather.6
  287.7 48.2 all-gather.8
  418.0 48.2 all-gather.10
